TPU v7x, 32 devices: a whole 2x2x4 slice. The times are simulated.
32 devices in a mesh: dp: 4 (over x, core), fsdp: 4 (over z), tensor: 2 (over y).
Axes of the slice: x: 2, y: 2, z: 4, core: 2. Of those that a mesh axis runs over, the one named last changes fastest.
Arguments:
- activations: bfloat16 [4096, 4096], P(('dp', 'tensor'), 'fsdp'), may hold values from -6 to 6
- cotangent: bfloat16 [4096, 16384], P('dp', 'tensor'), may hold values from -6 to 6
- weight: bfloat16 [4096, 16384], P('fsdp', 'tensor'), may hold values from -0.046875 to 0.046875
- residual: bfloat16 [4, 4096, 16384], P('dp', 'fsdp', 'tensor'), may hold values from -6 to 6
- step_size: float32 [1], replicated, may hold values from 0.02 to 0.06
- kept_blocks: int32 [4, 4, 2, 8], P('dp', 'fsdp', 'tensor'), may hold values from 0 to 511, as said below
Outputs:
- input_grad: bfloat16 [4096, 4096], P(('dp', 'tensor'), 'fsdp')
- residual_out: bfloat16 [4, 4096, 16384], P('dp', 'fsdp', 'tensor')
- owned: float32 [4, 4, 2, 128, 128, 128], P('dp', 'fsdp', 'tensor')
Inputs may be any that keep to these rules, and one draw needn't show every extreme that they name: The 8 entries of kept_blocks[a, f, t, :] are different block numbers.
All inputs are finite; a program needn't handle non-finite values.
Results may differ from a plain program's by a relative error of at most 0.0029.
Values may be sent and summed in bfloat16 or wider, within the bound.
No kernel may reach another device: no remote copies, remote signals or barrier semaphores. Data moves between devices by JAX's collectives and lax.ppermute only.
A program may use at most 128 MiB of HBM per device.

v0:
```python
import functools

import jax
import jax.numpy as jnp
from jax import lax
from jax.experimental import pallas as pl
from jax.experimental.pallas import tpu as pltpu
from jax.sharding import PartitionSpec as P

BLK = 128
MIB = 1024 * 1024
LABEL_ROWS = 16
RADIX = 16


def cost(flops, nbytes):
    return pl.CostEstimate(flops=flops, bytes_accessed=nbytes, transcendentals=0)


def params(mib=62):
    return pltpu.CompilerParams(vmem_limit_bytes=mib * MIB)


def dot_nt(a, b):
    return lax.dot_general(a, b, (((1,), (1,)), ((), ())), preferred_element_type=jnp.float32)


def dot_nn(a, b):
    return lax.dot_general(a, b, (((1,), (0,)), ((), ())), preferred_element_type=jnp.float32)


def chunking(cols):
    if cols < 8192:
        return cols // 2, 0, cols // 2
    return 1024, cols // 2048 - 1, 2048


def column_chunking(cols):
    if cols < 8192:
        return cols // 2, 0, cols // 2, [cols // 2]
    return 1024, cols // 1024 - 2, 1024, [512, 512]


def smem():
    return pl.BlockSpec(memory_space=pltpu.SMEM)


def vmem():
    return pl.BlockSpec(memory_space=pltpu.VMEM)


def hbm():
    return pl.BlockSpec(memory_space=pltpu.HBM)


def anywhere():
    return pl.BlockSpec(memory_space=pl.ANY)


def in_hbm(x):
    return pltpu.with_memory_space_constraint(x, pltpu.HBM)


def in_vmem(x):
    return pltpu.with_memory_space_constraint(x, pltpu.VMEM)


def cot_copies(here_ref, split, cot_ref, buf_ref, sems):
    if not split:
        return [pltpu.make_async_copy(cot_ref, buf_ref, sems.at[0])]
    half = buf_ref.shape[0] // 2
    copies = []
    for i, at in enumerate((here_ref[0], 1 - here_ref[0])):
        rows = pl.ds(pl.multiple_of(at * half, half), half)
        copies.append(pltpu.make_async_copy(cot_ref.at[rows], buf_ref.at[pl.ds(i * half, half)], sems.at[i]))
    return copies


def input_grad_kernel(split, zero_copies, here_ref, _, kept_in, cot_ref, w_ref, res_ref, *refs):
    if split:
        acts_ref, away_ref, acts_t_ref, *refs = refs
    own_ref, owned_ref, kept_cot_ref, kept_res_ref, cot_first_ref, res_first_ref, *refs = refs
    acc_ref, cot_head, w_head, cot_body, w_body, cot_tail, w_tail, zero_ref, *refs = refs
    kept_ref, kept_sem, cot_sem, w_sem, zero_sem, kept_cot_sem, kept_res_sem, first_sem, own_sem, *refs = refs
    zero_rows = zero_ref.shape[0]
    rows, hidden = w_ref.shape
    width = min(256, rows)
    keep = kept_cot_ref.shape[0]
    half = own_ref.shape[0]
    head, chunks, chunk = chunking(hidden)

    def loads(at, size, cot_buf, w_buf, i):
        part = pl.ds(at, size)
        return cot_copies(here_ref, split, cot_ref.at[:, part], cot_buf, cot_sem.at[i]) + [
            pltpu.make_async_copy(w_ref.at[:, part], w_buf, w_sem.at[i])
        ]

    def head_loads():
        return loads(0, head, cot_head, w_head, 0)

    def tail_loads():
        return loads(hidden - head, head, cot_tail, w_tail, 1)

    def body_loads(j):
        return loads(pl.multiple_of(head + j * chunk, BLK), chunk, cot_body.at[j], w_body.at[j], 2 + j)

    def start(copies):
        for copy in copies:
            copy.start()

    def wait(copies):
        for copy in copies:
            copy.wait()

    def side_copies():
        part = pl.ds(0, res_first_ref.shape[1])
        copies = cot_copies(here_ref, split, cot_ref.at[:, part], cot_first_ref, first_sem)
        copies.append(pltpu.make_async_copy(res_ref.at[:, part], res_first_ref, first_sem.at[2]))
        for z in range(zero_copies):
            part = pl.ds(z * zero_rows, zero_rows)
            copies.append(pltpu.make_async_copy(zero_ref, owned_ref.at[part], zero_sem.at[z]))
        for k in range(keep):
            col_blocks = hidden // BLK
            row = pl.ds(pl.multiple_of(kept_ref[k] // col_blocks * BLK, BLK), BLK)
            col = pl.ds(pl.multiple_of(kept_ref[k] % col_blocks * BLK, BLK), BLK)
            copies += cot_copies(here_ref, split, cot_ref.at[:, col], kept_cot_ref.at[k], kept_cot_sem.at[k])
            copies.append(pltpu.make_async_copy(res_ref.at[row, col], kept_res_ref.at[k], kept_res_sem.at[k]))
        return copies

    if split:
        acts_buf, acts_t_buf, away_buf, acts_sem, acts_t_sem, away_sem = refs
        acts_copy = pltpu.make_async_copy(acts_ref, acts_buf, acts_sem)
        acts_t_copy = pltpu.make_async_copy(acts_t_buf, acts_t_ref.at[:, pl.ds(0, half)], acts_t_sem)
        acts_copy.start()
    start(head_loads())
    kept_copy = pltpu.make_async_copy(kept_in, kept_ref, kept_sem)
    kept_copy.start()
    zero_ref[...] = jnp.zeros_like(zero_ref)
    if split:
        acts_copy.wait()
        acts_t_buf[...] = acts_buf[...].T
        acts_t_copy.start()
    start(body_loads(0) if chunks else tail_loads())
    wait(head_loads())
    kept_copy.wait()
    if chunks:
        start(body_loads(1))
    for at in range(0, rows, width):
        cols = slice(at, at + width)
        acc_ref[:, cols] = dot_nt(cot_head[...], w_head[cols, :])

    if chunks:

        @pl.loop(0, chunks)
        def _(j):
            wait(body_loads(j))

            @pl.when(j + 2 < chunks)
            def _():
                start(body_loads(j + 2))

            @pl.when(j + 2 == chunks)
            def _():
                start(tail_loads())
                start(side_copies())

            for at in range(0, rows, width):
                cols = slice(at, at + width)
                acc_ref[:, cols] += dot_nt(cot_body[j], w_body[j, cols, :])

    else:
        start(side_copies())
    wait(tail_loads())
    outputs = []
    for n, at in enumerate(range(0, rows, width)):
        cols = slice(at, at + width)
        total = acc_ref[:, cols] + dot_nt(cot_tail[...], w_tail[cols, :])
        if split:
            own_ref[:, cols] = total[:half]
            away_buf[:, cols] = total[half:].astype(jnp.bfloat16)
            outputs.append(pltpu.make_async_copy(away_buf.at[:, cols], away_ref.at[:, cols], away_sem.at[n]))
        else:
            acc_ref[:, cols] = total
            outputs.append(pltpu.make_async_copy(acc_ref.at[:, cols], own_ref.at[:, cols], own_sem.at[n]))
    start(outputs)
    if split:
        acts_t_copy.wait()
    wait(side_copies())
    wait(outputs)


def input_grad_partials(here, me, kept, cot, weight, residual, owned_count, acts):
    split = acts is not None
    tokens, cols = cot.shape
    rows = weight.shape[0]
    head, chunks, chunk = chunking(cols)
    first = column_chunking(cols)[0]
    keep = kept.shape[0]
    own_rows = tokens // 2 if split else tokens
    zero_rows = min(16, owned_count)
    zero_copies = owned_count // zero_rows
    out_shape = [
        pltpu.VMEM((own_rows, rows), jnp.float32) if split else jax.ShapeDtypeStruct((own_rows, rows), jnp.float32),
        pltpu.HBM((owned_count, BLK, BLK), jnp.float32),
        pltpu.VMEM((keep, tokens, BLK), jnp.bfloat16),
        pltpu.VMEM((keep, BLK, BLK), jnp.bfloat16),
        pltpu.VMEM((tokens, first), jnp.bfloat16),
        pltpu.VMEM((rows, first), jnp.bfloat16),
    ]
    out_specs = [vmem() if split else anywhere(), hbm()] + [vmem()] * 4
    scratch = [
        pltpu.VMEM((tokens, rows), jnp.float32),
        pltpu.VMEM((tokens, head), jnp.bfloat16),
        pltpu.VMEM((rows, head), jnp.bfloat16),
        pltpu.VMEM((max(chunks, 1), tokens, chunk), jnp.bfloat16),
        pltpu.VMEM((max(chunks, 1), rows, chunk), jnp.bfloat16),
        pltpu.VMEM((tokens, head), jnp.bfloat16),
        pltpu.VMEM((rows, head), jnp.bfloat16),
        pltpu.VMEM((zero_rows, BLK, BLK), jnp.float32),
        pltpu.SMEM(kept.shape, jnp.int32),
        pltpu.SemaphoreType.DMA,
        pltpu.SemaphoreType.DMA((chunks + 2, 2)),
        pltpu.SemaphoreType.DMA((chunks + 2,)),
        pltpu.SemaphoreType.DMA((zero_copies,)),
        pltpu.SemaphoreType.DMA((keep, 2)),
        pltpu.SemaphoreType.DMA((keep,)),
        pltpu.SemaphoreType.DMA((3,)),
        pltpu.SemaphoreType.DMA((4,)),
    ]
    if split:
        out_shape = [
            jax.ShapeDtypeStruct((own_rows, rows), jnp.bfloat16),
            pltpu.VMEM((rows, tokens), jnp.bfloat16),
        ] + out_shape
        out_specs = [anywhere(), vmem()] + out_specs
        scratch += [
            pltpu.VMEM(acts.shape, jnp.bfloat16),
            pltpu.VMEM((rows, own_rows), jnp.bfloat16),
            pltpu.VMEM((own_rows, rows), jnp.bfloat16),
            pltpu.SemaphoreType.DMA,
            pltpu.SemaphoreType.DMA,
            pltpu.SemaphoreType.DMA((4,)),
        ]
    return pl.pallas_call(
        functools.partial(input_grad_kernel, split, zero_copies),
        out_shape=out_shape,
        in_specs=[smem()] * 2 + [hbm()] * (4 + split),
        out_specs=out_specs,
        scratch_shapes=scratch,
        compiler_params=params(43),
        cost_estimate=cost(2 * tokens * rows * cols, 2 * cols * (tokens + rows) + 4 * owned_count * BLK * BLK),
        name="input_grad_partials",
    )(here, me, in_hbm(kept), in_hbm(cot), in_hbm(weight), in_hbm(residual), *([in_hbm(acts)] if split else []))


def kept_kernel(pair, col_blocks, kept_ref, step_ref, *refs):
    if pair:
        _, *refs = refs
    act_ref, cot_ref, res_ref, acts_t_ref, out_ref = refs
    keep = cot_ref.shape[0]
    acts_t_ref[:, acts_t_ref.shape[1] - act_ref.shape[0] :] = act_ref[...].T
    for k in range(keep):
        row = pl.ds(pl.multiple_of(kept_ref[k] // col_blocks * BLK, BLK), BLK)
        gradient = dot_nn(acts_t_ref[row, :], cot_ref[k])
        out_ref[k * BLK : (k + 1) * BLK, :] = (res_ref[k].astype(jnp.float32) + step_ref[0] * gradient).astype(
            jnp.bfloat16
        )
    lane = lax.broadcasted_iota(jnp.int32, (LABEL_ROWS, BLK), 1) % keep
    low = lax.broadcasted_iota(jnp.int32, (LABEL_ROWS, BLK), 0) % 2 == 1
    label = jnp.zeros((LABEL_ROWS, BLK), jnp.int32)
    for k in range(keep):
        digit = jnp.where(low, kept_ref[k] % RADIX, kept_ref[k] // RADIX)
        label = jnp.where(lane == k, digit, label)
    out_ref[keep * BLK :, :] = label.astype(jnp.float32).astype(jnp.bfloat16)


def kept_blocks_of(kept, step_size, acts_t, act, kept_cot, kept_res, col_blocks):
    rows = act.shape[1]
    keep, tokens = kept_cot.shape[:2]
    pair = acts_t is not None
    return pl.pallas_call(
        functools.partial(kept_kernel, pair, col_blocks),
        out_shape=[
            pltpu.VMEM((rows, tokens), jnp.bfloat16),
            jax.ShapeDtypeStruct((keep * BLK + LABEL_ROWS, BLK), jnp.bfloat16),
        ],
        in_specs=[smem()] * 2 + [vmem()] * (3 + pair),
        out_specs=[vmem(), vmem()],
        input_output_aliases={2: 0} if pair else {},
        compiler_params=params(4),
        cost_estimate=cost(2 * tokens * BLK * BLK * keep, 4 * tokens * rows + 2 * keep * tokens * BLK),
        name="kept_blocks",
    )(kept, step_size, *([in_vmem(acts_t)] if pair else []), in_vmem(act), in_vmem(kept_cot), in_vmem(kept_res))


def residual_kernel(split, here_ref, step_ref, acts_t_ref, cot_first, res_first, cot_ref, res_ref, out_ref, *refs):
    first_out, cot_body, res_body, cot_tail, res_tail, cot_sem, res_sem, out_sem = refs
    step = step_ref[0]
    first, chunks, chunk, tails = column_chunking(cot_ref.shape[1])

    def loads(at, cot_buf, res_buf, i):
        part = pl.ds(at, res_buf.shape[1])
        return cot_copies(here_ref, split, cot_ref.at[:, part], cot_buf, cot_sem.at[i]) + [
            pltpu.make_async_copy(res_ref.at[:, part], res_buf, res_sem.at[i])
        ]

    def store(at, res_buf, i):
        return pltpu.make_async_copy(res_buf, out_ref.at[:, pl.ds(at, res_buf.shape[1])], out_sem.at[i])

    def body_at(j):
        return pl.multiple_of(first + j * chunk, BLK)

    def body_loads(j):
        return loads(body_at(j), cot_body.at[j], res_body.at[j], j)

    def body_store(j):
        return store(body_at(j), res_body.at[j], j)

    def tail_at(t):
        return first + chunks * chunk + sum(tails[:t])

    def tail_loads(t):
        return loads(tail_at(t), cot_tail.at[t], res_tail.at[t], chunks + t)

    def tail_store(t):
        return store(tail_at(t), res_tail.at[t], chunks + t)

    def start(copies):
        for copy in copies:
            copy.start()

    def wait(copies):
        for copy in copies:
            copy.wait()

    def start_tails():
        for t in range(len(tails)):
            start(tail_loads(t))

    def work(cot_buf, res_buf, out_buf):
        size = res_buf.shape[1]
        width = min(256, size)
        for at in range(0, size, width):
            part = slice(at, at + width)
            gradient = dot_nn(acts_t_ref[...], cot_buf[:, part])
            out_buf[:, part] = (res_buf[:, part].astype(jnp.float32) + step * gradient).astype(jnp.bfloat16)

    if chunks:
        start(body_loads(0))
    else:
        start_tails()
    work(cot_first, res_first, first_out)
    first_store = store(0, first_out, chunks + len(tails))
    first_store.start()

    if chunks:
        start(body_loads(1))

        @pl.loop(0, chunks)
        def _(j):
            wait(body_loads(j))

            @pl.when(j + 2 < chunks)
            def _():
                start(body_loads(j + 2))

            @pl.when(j + 2 == chunks)
            def _():
                start_tails()

            work(cot_body.at[j], res_body.at[j], res_body.at[j])
            body_store(j).start()

    for t in range(len(tails)):
        wait(tail_loads(t))
        work(cot_tail.at[t], res_tail.at[t], res_tail.at[t])
        tail_store(t).start()
    first_store.wait()
    for j in range(chunks):
        body_store(j).wait()
    for t in range(len(tails)):
        tail_store(t).wait()


def residual_of(here, step_size, acts_t, cot_first, res_first, cot, residual, split):
    tokens, cols = cot.shape
    rows = residual.shape[0]
    first, chunks, chunk, tails = column_chunking(cols)
    parts = chunks + len(tails)
    return pl.pallas_call(
        functools.partial(residual_kernel, split),
        out_shape=pltpu.HBM((rows, cols), jnp.bfloat16),
        in_specs=[smem()] * 2 + [vmem()] * 3 + [hbm()] * 2,
        out_specs=hbm(),
        scratch_shapes=[
            pltpu.VMEM((rows, first), jnp.bfloat16),
            pltpu.VMEM((max(chunks, 1), tokens, chunk), jnp.bfloat16),
            pltpu.VMEM((max(chunks, 1), rows, chunk), jnp.bfloat16),
            pltpu.VMEM((len(tails), tokens, tails[0]), jnp.bfloat16),
            pltpu.VMEM((len(tails), rows, tails[0]), jnp.bfloat16),
            pltpu.SemaphoreType.DMA((parts, 2)),
            pltpu.SemaphoreType.DMA((parts,)),
            pltpu.SemaphoreType.DMA((parts + 1,)),
        ],
        compiler_params=params(36),
        cost_estimate=cost(2 * tokens * rows * cols, 2 * tokens * (rows + cols) + 4 * rows * cols),
        name="residual_out",
    )(
        here,
        step_size,
        in_vmem(acts_t),
        in_vmem(cot_first),
        in_vmem(res_first),
        in_hbm(cot),
        in_hbm(residual),
    )


def finish_kernel(groups, keep, pair, col_blocks, me_ref, kept_ref, *refs):
    if pair:
        own_ref, arrived_ref, *refs = refs
    block_refs = refs[:groups]
    refs = refs[groups + 2 :]
    if pair:
        grad_ref, *refs = refs
    out_ref, res_ref, sum_ref, table_ref, scalar_ref, zero_ref, sem, table_sem, zero_sem, *refs = refs
    total = groups * keep
    me = me_ref[0]

    zero_ref[...] = jnp.zeros_like(zero_ref)
    zero_copies = []
    for k in range(keep):
        at = pl.multiple_of(kept_ref[k] // col_blocks * BLK, BLK)
        col = pl.multiple_of(kept_ref[k] % col_blocks * BLK, BLK)
        zero_copies.append(
            pltpu.make_async_copy(zero_ref, res_ref.at[pl.ds(at, BLK), pl.ds(col, BLK)], zero_sem.at[k])
        )
        zero_copies[k].start()

    row = lax.broadcasted_iota(jnp.int32, (total, BLK), 0)
    lane = lax.broadcasted_iota(jnp.int32, (total, BLK), 1)
    numbers = jnp.full((total, BLK), -1, jnp.int32)
    for g, block_ref in enumerate(block_refs):
        digits = block_ref[keep * BLK :, :].astype(jnp.float32).astype(jnp.int32)
        numbers = jnp.where(lane // keep == g, digits[0:1, :] * RADIX + digits[1:2, :], numbers)
    numbers = numbers.astype(jnp.float32)
    number = jnp.sum(jnp.where(lane == row, numbers, 0.0), axis=1, keepdims=True)
    first = jnp.min(jnp.where(numbers == number, lane.astype(jnp.float32), float(BLK)), axis=1, keepdims=True)
    final = jnp.max(jnp.where(numbers == number, lane.astype(jnp.float32), -1.0), axis=1, keepdims=True)
    number = jnp.broadcast_to(number, (total, BLK)).astype(jnp.int32)
    first = jnp.broadcast_to(first, (total, BLK)).astype(jnp.int32)
    first = jnp.where(number % groups == me, first, -1)
    final = jnp.broadcast_to(final, (total, BLK)).astype(jnp.int32)
    table_ref[...] = jnp.where(lane == 0, first, jnp.where(lane == 1, number // groups, final))
    table = pltpu.make_async_copy(table_ref, scalar_ref, table_sem)
    table.start()

    grad_copies = []
    if pair:
        grad_buf, grad_sem = refs
        size = grad_buf.shape[0] // grad_sem.shape[0]
        for c in range(grad_sem.shape[0]):
            part = slice(c * size, (c + 1) * size)
            grad_buf[part, :] = (own_ref[part, :] + arrived_ref[part, :].astype(jnp.float32)).astype(jnp.bfloat16)
            grad_copies.append(pltpu.make_async_copy(grad_buf.at[part, :], grad_ref.at[part, :], grad_sem.at[c]))
            grad_copies[c].start()

    table.wait()

    def copy(i):
        return pltpu.make_async_copy(sum_ref.at[i], out_ref.at[scalar_ref[i, 1]], sem.at[i])

    def block(i):
        at = i % keep * BLK
        return block_refs[i // keep][at : at + BLK, :].astype(jnp.float32)

    for i in range(total):
        slot = scalar_ref[i, 0]

        @pl.when(slot >= 0)
        def _(i=i, slot=slot):
            @pl.when(slot == i)
            def _():
                sum_ref[i] = block(i)

            if i >= keep:

                @pl.when(slot < i)
                def _():
                    sum_ref[slot] += block(i)

            @pl.when(scalar_ref[i, 2] == i)
            def _():
                copy(slot).start()

    for done in zero_copies + grad_copies:
        done.wait()
    for i in range(total):

        @pl.when(scalar_ref[i, 0] == i)
        def _(i=i):
            copy(i).wait()


def finish(me, kept, parts, blocks, zeros, residual):
    groups = len(blocks)
    keep = kept.shape[0]
    out_shape = [pltpu.HBM(a.shape, a.dtype) for a in (zeros, residual)]
    out_specs = [hbm(), hbm()]
    scratch = [
        pltpu.VMEM((groups * keep, BLK, BLK), jnp.float32),
        pltpu.VMEM((groups * keep, BLK), jnp.int32),
        pltpu.SMEM((groups * keep, BLK), jnp.int32),
        pltpu.VMEM((BLK, BLK), jnp.bfloat16),
        pltpu.SemaphoreType.DMA((groups * keep,)),
        pltpu.SemaphoreType.DMA,
        pltpu.SemaphoreType.DMA((keep,)),
    ]
    if parts:
        out_shape.insert(0, pltpu.HBM(parts[0].shape, jnp.bfloat16))
        out_specs.insert(0, hbm())
        scratch += [pltpu.VMEM(parts[0].shape, jnp.bfloat16), pltpu.SemaphoreType.DMA((4,))]
        parts = [in_vmem(parts[0]), parts[1]]
    first = 2 + len(parts) + groups
    return pl.pallas_call(
        functools.partial(finish_kernel, groups, keep, bool(parts), residual.shape[1] // BLK),
        out_shape=out_shape,
        in_specs=[smem(), smem()] + [vmem()] * (len(parts) + groups) + [hbm(), hbm()],
        out_specs=out_specs,
        scratch_shapes=scratch,
        input_output_aliases={first: len(out_shape) - 2, first + 1: len(out_shape) - 1},
        compiler_params=params(10),
        cost_estimate=cost(groups * keep * BLK * BLK, groups * keep * BLK * BLK * 8),
        name="finish",
    )(me, kept, *parts, *blocks, in_hbm(zeros), in_hbm(residual))


def swapped(x, axis, mask):
    return lax.ppermute(x, axis, [(i, i ^ mask) for i in range(lax.axis_size(axis))])


def of_all_groups(x):
    return [x] + [swapped(x, "dp", mask) for mask in range(1, lax.axis_size("dp"))]


def body(activations, cotangent, weight, residual, step_size, kept_blocks):
    rows, cols = weight.shape
    groups = lax.axis_size("dp")
    owned_count = (rows // BLK) * (cols // BLK) // groups
    kept = kept_blocks.reshape(-1)
    me = lax.axis_index("dp").astype(jnp.int32).reshape(1)
    here = lax.axis_index("tensor").astype(jnp.int32).reshape(1)
    pair = lax.axis_size("tensor") == 2
    if pair:
        act = swapped(activations, "tensor", 1)
        away, acts_t, own, zeros, kept_cot, kept_res, cot_first, res_first = input_grad_partials(
            here, me, kept, cotangent, weight, residual[0], owned_count, activations
        )
        parts = [own, swapped(away, "tensor", 1)]
    else:
        act = lax.all_gather(activations, "tensor", axis=0, tiled=True)
        acts_t = None
        own, zeros, kept_cot, kept_res, cot_first, res_first = input_grad_partials(
            here, me, kept, cotangent, weight, residual[0], owned_count, None
        )
        summed = lax.psum_scatter(own, "tensor", scatter_dimension=0, tiled=True)
        parts = []
    acts_t, blocks = kept_blocks_of(kept, step_size, acts_t, act, kept_cot, kept_res, cols // BLK)
    all_blocks = of_all_groups(blocks)
    rounded = residual_of(here, step_size, acts_t, cot_first, res_first, cotangent, residual[0], pair)
    *grads, owned, residual_out = finish(me, kept, parts, all_blocks, zeros, rounded)
    input_grad = grads[0] if pair else summed.astype(jnp.bfloat16)
    return (input_grad, residual_out[None], owned.reshape(1, 1, 1, owned_count, BLK, BLK))


def solution(mesh):
    in_specs = (
        P(("dp", "tensor"), "fsdp"),
        P("dp", "tensor"),
        P("fsdp", "tensor"),
        P("dp", "fsdp", "tensor"),
        P(),
        P("dp", "fsdp", "tensor", None),
    )
    out_specs = (
        P(("dp", "tensor"), "fsdp"),
        P("dp", "fsdp", "tensor"),
        P("dp", "fsdp", "tensor", None, None, None),
    )
    return jax.shard_map(body, mesh=mesh, in_specs=in_specs, out_specs=out_specs, check_vma=False)
```

profile of v0, /device:TPU:1, one launch (start us, length us, event | category | flops | bytes accessed | tf_op | source)
XLA Modules:
  0.0 54.7 jit_solution(11687452949664355604)
XLA Ops:
  0.6 2.1 %collective-permute-start.1 = (bf16[512,1024]{1,0:T(8,128)(2,1)}, bf16[512,1024]{1,0:T(8,128)(2,1)S(1)}, u32[]{:S(2)}, u32[]{:S(2)}) collective-permute-start(bf16[512,1024]{1,0:T(8,128)(2,1)} %refs_0_.1), channel_id=1, source_target_pairs={{0,1},{1,0},{2,3},{3,2},{4,5},{5,4},{6,7},{7,6},{8,9},{9,8},{10,11... | collective-permute-start | bytes 3145736 | tf_op jit(solution)/shard_map/ppermute | solution.py:539
  2.8 0.0 copy-start
  2.8 23.2 %input_grad_partials.1 = (bf16[512,1024]{1,0:T(8,128)(2,1)}, bf16[1024,1024]{1,0:T(8,128)(2,1)S(1)}, f32[512,1024]{1,0:T(8,128)S(1)}, f32[128,128,128]{2,1,0:T(8...) custom-call(s32[1]{0:T(128)} %bitcast.2.here_ref, ...), custom_call_target="tpu_custom_call" | custom-call | flops 17179869184 | bytes 41943040 | tf_op jit(solution)/shard_map/input_grad_partials/pallas_call | solution.py:244
  26.0 0.1 collective-permute-start
  26.7 0.0 collective-permute-done.1.refs_1_
  26.8 0.0 copy-done
  26.8 1.6 %kept_blocks.1 = (bf16[1024,1024]{1,0:T(8,128)(2,1)S(1)}, bf16[1040,128]{1,0:T(8,128)(2,1)S(1)}) custom-call(s32[8]{0:T(128)S(1)} %bitcast.7, f32[1]{0:T(128)S(6)} %copy.15.step_ref, bf16[1024,1024]{1,0:T(8,128)(2,1)S(1)} %get-tuple-element.18.refs_0_, bf16[512,1024]{1,0:T(8,128)(2,1)S(1)} %collective-permute-done.1.refs_1_, ...), custom_call_target="tpu_custom_call", output_to_operand_aliasing={{0}: (2, {})} | custom-call | flops 268435456 | bytes 6291456 | tf_op jit(solution)/shard_map/kept_blocks/pallas_call | solution.py:281
  28.3 2.6 %collective-permute-start.4 = (bf16[1040,128]{1,0:T(8,128)(2,1)S(1)}, bf16[1040,128]{1,0:T(8,128)(2,1)S(1)}, u32[]{:S(2)}, u32[]{:S(2)}) collective-permute-start(bf16[1040,128]{1,0:T(8,128)(2,1)S(1)} %get-tuple-element.21.refs_2_), channel_id=1, source_target_pairs={{0,24},{8,16},{16,8},{24,0},{1,25},{9,17},{17,9},{25,1},{2,26},{10... | collective-permute-start | bytes 798728 | tf_op jit(solution)/shard_map/ppermute | solution.py:539
  30.9 0.0 collective-permute-start.3
  30.9 0.5 collective-permute-start.2
  31.4 20.6 %residual_out.1.refs_7_ = bf16[1024,8192]{1,0:T(8,128)(2,1)} custom-call(s32[1]{0:T(128)} %bitcast.2.here_ref, f32[1]{0:T(128)S(6)} %copy.15.step_ref, bf16[1024,1024]{1,0:T(8,128)(2,1)S(1)} %get-tuple-element.23.acts_t_ref, bf16[1024,1024]{1,0:T(8,128)(2,1)S(1)} %get-tuple-element.24.cot_first, bf16[1024,1024]{1,0:T(8,128)(2,1)S(1)} %get-tuple-element.25.res_first, ...), custom_call_target="tpu_custom_call" | custom-call | flops 17179869184 | bytes 52428800 | tf_op jit(solution)/shard_map/residual_out/pallas_call | solution.py:390
  52.0 0.0 collective-permute-done.refs_1_
  52.0 0.0 collective-permute-done.4.refs_5_
  52.0 0.0 collective-permute-done.3.refs_4_
  52.0 0.0 collective-permute-done.2.refs_3_
  52.0 2.5 %finish.1 = (bf16[512,1024]{1,0:T(8,128)(2,1)}, f32[128,128,128]{2,1,0:T(8,128)}, bf16[1024,8192]{1,0:T(8,128)(2,1)}) custom-call(s32[1]{0:T(128)} %bitcast._.me_ref, s32[8]{0:T(128)S(1)} %bitcast.8, f32[512,1024]{1,0:T(8,128)S(1)} %get-tuple-element.16.refs_0_, ...), custom_call_target="tpu_custom_call", output_to_operand_aliasing={{1}: (8, {}), {2}: (9, {})} | custom-call | flops 524288 | bytes 4194304 | tf_op jit(solution)/shard_map/finish/pallas_call | solution.py:525
Async XLA Ops:
  0.6 26.1 %collective-permute-start.1 = (bf16[512,1024]{1,0:T(8,128)(2,1)}, bf16[512,1024]{1,0:T(8,128)(2,1)S(1)}, u32[]{:S(2)}, u32[]{:S(2)}) collective-permute-start(bf16[512,1024]{1,0:T(8,128)(2,1)} %refs_0_.1), channel_id=1, source_target_pairs={{0,1},{1,0},{2,3},{3,2},{4,5},{5,4},{6,7},{7,6},{8,9},{9,8},{10,11... | collective-permute-start | bytes 3145736 | tf_op jit(solution)/shard_map/ppermute | solution.py:539
  2.8 24.0 %copy-start = (s32[1,1,1,8]{3,2,1,0:T(1,128)S(1)}, s32[1,1,1,8]{3,2,1,0:T(1,128)}, u32[]{:S(2)}) copy-start(s32[1,1,1,8]{3,2,1,0:T(1,128)} %param.11) | copy-start | bytes 100
  26.0 26.0 %collective-permute-start = (bf16[512,1024]{1,0:T(8,128)(2,1)}, bf16[512,1024]{1,0:T(8,128)(2,1)S(1)}, u32[]{:S(2)}, u32[]{:S(2)}) collective-permute-start(bf16[512,1024]{1,0:T(8,128)(2,1)} %get-tuple-element.17), channel_id=1, source_target_pairs={{0,1},{1,0},{2,3},{3,2},{4,5},{5,4},{6,7},{7,6},{8,9},{9,8},{10,11... | collective-permute-start | bytes 3145736 | tf_op jit(solution)/shard_map/ppermute | solution.py:539
  28.3 23.7 %collective-permute-start.4 = (bf16[1040,128]{1,0:T(8,128)(2,1)S(1)}, bf16[1040,128]{1,0:T(8,128)(2,1)S(1)}, u32[]{:S(2)}, u32[]{:S(2)}) collective-permute-start(bf16[1040,128]{1,0:T(8,128)(2,1)S(1)} %get-tuple-element.21.refs_2_), channel_id=1, source_target_pairs={{0,24},{8,16},{16,8},{24,0},{1,25},{9,17},{17,9},{25,1},{2,26},{10... | collective-permute-start | bytes 798728 | tf_op jit(solution)/shard_map/ppermute | solution.py:539
  30.9 21.1 %collective-permute-start.3 = (bf16[1040,128]{1,0:T(8,128)(2,1)S(1)}, bf16[1040,128]{1,0:T(8,128)(2,1)S(1)}, u32[]{:S(2)}, u32[]{:S(2)}) collective-permute-start(bf16[1040,128]{1,0:T(8,128)(2,1)S(1)} %get-tuple-element.21.refs_2_), channel_id=1, source_target_pairs={{0,16},{8,24},{16,0},{24,8},{1,17},{9,25},{17,1},{25,9},{2,18},{10... | collective-permute-start | bytes 798728 | tf_op jit(solution)/shard_map/ppermute | solution.py:539
  30.9 21.1 %collective-permute-start.2 = (bf16[1040,128]{1,0:T(8,128)(2,1)S(1)}, bf16[1040,128]{1,0:T(8,128)(2,1)S(1)}, u32[]{:S(2)}, u32[]{:S(2)}) collective-permute-start(bf16[1040,128]{1,0:T(8,128)(2,1)S(1)} %get-tuple-element.21.refs_2_), channel_id=1, source_target_pairs={{0,8},{8,0},{16,24},{24,16},{1,9},{9,1},{17,25},{25,17},{2,10},{10... | collective-permute-start | bytes 798728 | tf_op jit(solution)/shard_map/ppermute | solution.py:539
where the time goes:
time: 55.5 us; the launch traced here: 54.7 us
  Pallas kernels  47.9 us (86%)
  starting transfers between devices  5.29 us (10%)
  between operations  1.51 us (3%)
    pallas_call x1, Pallas kernels, input_grad_partials(): pl.pallas_call(functools.partial(input_grad_kernel, split, zero_copies),...  23.2 us
    pallas_call x1, Pallas kernels, residual_of(): pl.pallas_call(functools.partial(residual_kernel, split), out_shape=pltpu...  20.6 us
    ppermute x5, starting transfers between devices, swapped(): lax.ppermute(x, axis, [(i, i ^ mask) for i in range(lax.axis_size(axis))])  5.29 us
    pallas_call x1, Pallas kernels, finish(): pl.pallas_call(functools.partial(finish_kernel, groups, keep, bool(parts)...  2.51 us
    pallas_call x1, Pallas kernels, kept_blocks_of(): pl.pallas_call(functools.partial(kept_kernel, pair, col_blocks), out_shap...  1.58 us
  transfers between devices with their start and end apart: 5, of which 0 were waited for; matrix products, arithmetic and copies ran while one was open for 0% of the time, Pallas kernels for 83%

commit v1 on v0

--- a/solution.py
+++ b/solution.py
@@ -33,12 +33,6 @@
     if cols < 8192:
         return cols // 2, 0, cols // 2
     return 1024, cols // 2048 - 1, 2048
-
-
-def column_chunking(cols):
-    if cols < 8192:
-        return cols // 2, 0, cols // 2, [cols // 2]
-    return 1024, cols // 1024 - 2, 1024, [512, 512]
 
 
 def smem():
@@ -79,9 +73,9 @@
 def input_grad_kernel(split, zero_copies, here_ref, _, kept_in, cot_ref, w_ref, res_ref, *refs):
     if split:
         acts_ref, away_ref, acts_t_ref, *refs = refs
-    own_ref, owned_ref, kept_cot_ref, kept_res_ref, cot_first_ref, res_first_ref, *refs = refs
+    own_ref, owned_ref, kept_cot_ref, kept_res_ref, *refs = refs
     acc_ref, cot_head, w_head, cot_body, w_body, cot_tail, w_tail, zero_ref, *refs = refs
-    kept_ref, kept_sem, cot_sem, w_sem, zero_sem, kept_cot_sem, kept_res_sem, first_sem, own_sem, *refs = refs
+    kept_ref, kept_sem, cot_sem, w_sem, zero_sem, kept_cot_sem, kept_res_sem, own_sem, *refs = refs
     zero_rows = zero_ref.shape[0]
     rows, hidden = w_ref.shape
     width = min(256, rows)
@@ -113,9 +107,7 @@
             copy.wait()
 
     def side_copies():
-        part = pl.ds(0, res_first_ref.shape[1])
-        copies = cot_copies(here_ref, split, cot_ref.at[:, part], cot_first_ref, first_sem)
-        copies.append(pltpu.make_async_copy(res_ref.at[:, part], res_first_ref, first_sem.at[2]))
+        copies = []
         for z in range(zero_copies):
             part = pl.ds(z * zero_rows, zero_rows)
             copies.append(pltpu.make_async_copy(zero_ref, owned_ref.at[part], zero_sem.at[z]))
@@ -194,7 +186,6 @@
     tokens, cols = cot.shape
     rows = weight.shape[0]
     head, chunks, chunk = chunking(cols)
-    first = column_chunking(cols)[0]
     keep = kept.shape[0]
     own_rows = tokens // 2 if split else tokens
     zero_rows = min(16, owned_count)
@@ -204,10 +195,8 @@
         pltpu.HBM((owned_count, BLK, BLK), jnp.float32),
         pltpu.VMEM((keep, tokens, BLK), jnp.bfloat16),
         pltpu.VMEM((keep, BLK, BLK), jnp.bfloat16),
-        pltpu.VMEM((tokens, first), jnp.bfloat16),
-        pltpu.VMEM((rows, first), jnp.bfloat16),
     ]
-    out_specs = [vmem() if split else anywhere(), hbm()] + [vmem()] * 4
+    out_specs = [vmem() if split else anywhere(), hbm()] + [vmem()] * 2
     scratch = [
         pltpu.VMEM((tokens, rows), jnp.float32),
         pltpu.VMEM((tokens, head), jnp.bfloat16),
@@ -224,7 +213,6 @@
         pltpu.SemaphoreType.DMA((zero_copies,)),
         pltpu.SemaphoreType.DMA((keep, 2)),
         pltpu.SemaphoreType.DMA((keep,)),
-        pltpu.SemaphoreType.DMA((3,)),
         pltpu.SemaphoreType.DMA((4,)),
     ]
     if split:
@@ -253,11 +241,16 @@
     )(here, me, in_hbm(kept), in_hbm(cot), in_hbm(weight), in_hbm(residual), *([in_hbm(acts)] if split else []))
 
 
-def kept_kernel(pair, col_blocks, kept_ref, step_ref, *refs):
+def kept_kernel(pair, col_blocks, here_ref, kept_ref, step_ref, cot_in, res_in, *refs):
     if pair:
         _, *refs = refs
-    act_ref, cot_ref, res_ref, acts_t_ref, out_ref = refs
+    act_ref, cot_ref, res_ref, acts_t_ref, out_ref, cot_first, res_first, first_sem = refs
     keep = cot_ref.shape[0]
+    part = pl.ds(0, res_first.shape[1])
+    copies = cot_copies(here_ref, pair, cot_in.at[:, part], cot_first, first_sem)
+    copies.append(pltpu.make_async_copy(res_in.at[:, part], res_first, first_sem.at[2]))
+    for copy in copies:
+        copy.start()
     acts_t_ref[:, acts_t_ref.shape[1] - act_ref.shape[0] :] = act_ref[...].T
     for k in range(keep):
         row = pl.ds(pl.multiple_of(kept_ref[k] // col_blocks * BLK, BLK), BLK)
@@ -272,31 +265,48 @@
         digit = jnp.where(low, kept_ref[k] % RADIX, kept_ref[k] // RADIX)
         label = jnp.where(lane == k, digit, label)
     out_ref[keep * BLK :, :] = label.astype(jnp.float32).astype(jnp.bfloat16)
-
-
-def kept_blocks_of(kept, step_size, acts_t, act, kept_cot, kept_res, col_blocks):
-    rows = act.shape[1]
+    for copy in copies:
+        copy.wait()
+
+
+def kept_blocks_of(here, kept, step_size, cot, residual, acts_t, act, kept_cot, kept_res):
+    rows, cols = residual.shape
+    first = chunking(cols)[0]
     keep, tokens = kept_cot.shape[:2]
     pair = acts_t is not None
     return pl.pallas_call(
-        functools.partial(kept_kernel, pair, col_blocks),
+        functools.partial(kept_kernel, pair, cols // BLK),
         out_shape=[
             pltpu.VMEM((rows, tokens), jnp.bfloat16),
             jax.ShapeDtypeStruct((keep * BLK + LABEL_ROWS, BLK), jnp.bfloat16),
+            pltpu.VMEM((tokens, first), jnp.bfloat16),
+            pltpu.VMEM((rows, first), jnp.bfloat16),
         ],
-        in_specs=[smem()] * 2 + [vmem()] * (3 + pair),
-        out_specs=[vmem(), vmem()],
-        input_output_aliases={2: 0} if pair else {},
+        in_specs=[smem()] * 3 + [hbm()] * 2 + [vmem()] * (3 + pair),
+        out_specs=[vmem()] * 4,
+        scratch_shapes=[pltpu.SemaphoreType.DMA((3,))],
+        input_output_aliases={5: 0} if pair else {},
         compiler_params=params(4),
         cost_estimate=cost(2 * tokens * BLK * BLK * keep, 4 * tokens * rows + 2 * keep * tokens * BLK),
         name="kept_blocks",
-    )(kept, step_size, *([in_vmem(acts_t)] if pair else []), in_vmem(act), in_vmem(kept_cot), in_vmem(kept_res))
+    )(
+        here,
+        kept,
+        step_size,
+        in_hbm(cot),
+        in_hbm(residual),
+        *([in_vmem(acts_t)] if pair else []),
+        in_vmem(act),
+        in_vmem(kept_cot),
+        in_vmem(kept_res),
+    )
 
 
 def residual_kernel(split, here_ref, step_ref, acts_t_ref, cot_first, res_first, cot_ref, res_ref, out_ref, *refs):
     first_out, cot_body, res_body, cot_tail, res_tail, cot_sem, res_sem, out_sem = refs
     step = step_ref[0]
-    first, chunks, chunk, tails = column_chunking(cot_ref.shape[1])
+    first, chunks, chunk = chunking(cot_ref.shape[1])
+    tails = [first]
 
     def loads(at, cot_buf, res_buf, i):
         part = pl.ds(at, res_buf.shape[1])
@@ -385,7 +395,8 @@
 def residual_of(here, step_size, acts_t, cot_first, res_first, cot, residual, split):
     tokens, cols = cot.shape
     rows = residual.shape[0]
-    first, chunks, chunk, tails = column_chunking(cols)
+    first, chunks, chunk = chunking(cols)
+    tails = [first]
     parts = chunks + len(tails)
     return pl.pallas_call(
         functools.partial(residual_kernel, split),
@@ -553,19 +564,21 @@
     pair = lax.axis_size("tensor") == 2
     if pair:
         act = swapped(activations, "tensor", 1)
-        away, acts_t, own, zeros, kept_cot, kept_res, cot_first, res_first = input_grad_partials(
+        away, acts_t, own, zeros, kept_cot, kept_res = input_grad_partials(
             here, me, kept, cotangent, weight, residual[0], owned_count, activations
         )
         parts = [own, swapped(away, "tensor", 1)]
     else:
         act = lax.all_gather(activations, "tensor", axis=0, tiled=True)
         acts_t = None
-        own, zeros, kept_cot, kept_res, cot_first, res_first = input_grad_partials(
+        own, zeros, kept_cot, kept_res = input_grad_partials(
             here, me, kept, cotangent, weight, residual[0], owned_count, None
         )
         summed = lax.psum_scatter(own, "tensor", scatter_dimension=0, tiled=True)
         parts = []
-    acts_t, blocks = kept_blocks_of(kept, step_size, acts_t, act, kept_cot, kept_res, cols // BLK)
+    acts_t, blocks, cot_first, res_first = kept_blocks_of(
+        here, kept, step_size, cotangent, residual[0], acts_t, act, kept_cot, kept_res
+    )
     all_blocks = of_all_groups(blocks)
     rounded = residual_of(here, step_size, acts_t, cot_first, res_first, cotangent, residual[0], pair)
     *grads, owned, residual_out = finish(me, kept, parts, all_blocks, zeros, rounded)

time: 55.5 us -> 57.7 us (1.040)
  Pallas kernels: 47.9 us -> 50.2 us
    pallas_call x1, Pallas kernels: 1.58 us -> 3.71 us  [kept_blocks_of(): pl.pallas_call(functools.partial(kept_kernel, pair, cols // BLK), out_sha...]
    pallas_call x1, Pallas kernels: 20.6 us -> 21.6 us  [residual_of(): pl.pallas_call(functools.partial(residual_kernel, split), out_shape=pltpu...]
    pallas_call x1, Pallas kernels: 23.2 us -> 22.4 us  [input_grad_partials(): pl.pallas_call(functools.partial(input_grad_kernel, split, zero_copies),...]
  transfers between devices with their start and end apart: 5 -> 5, of which waited for: 0 -> 0; matrix products, arithmetic and copies ran while one was open for 0% -> 0% of each run, Pallas kernels for 83% -> 84%
where the time goes in v1:
time: 57.7 us; the launch traced here: 57 us
  Pallas kernels  50.2 us (87%)
  starting transfers between devices  5.3 us (9%)
  between operations  1.52 us (3%)
    pallas_call x1, Pallas kernels, input_grad_partials(): pl.pallas_call(functools.partial(input_grad_kernel, split, zero_copies),...  22.4 us
    pallas_call x1, Pallas kernels, residual_of(): pl.pallas_call(functools.partial(residual_kernel, split), out_shape=pltpu...  21.6 us
    ppermute x5, starting transfers between devices, swapped(): lax.ppermute(x, axis, [(i, i ^ mask) for i in range(lax.axis_size(axis))])  5.3 us
    pallas_call x1, Pallas kernels, kept_blocks_of(): pl.pallas_call(functools.partial(kept_kernel, pair, cols // BLK), out_sha...  3.71 us
    pallas_call x1, Pallas kernels, finish(): pl.pallas_call(functools.partial(finish_kernel, groups, keep, bool(parts)...  2.51 us
  transfers between devices with their start and end apart: 5, of which 0 were waited for; matrix products, arithmetic and copies ran while one was open for 0% of the time, Pallas kernels for 84%

profile of v1, /device:TPU:1, one launch (start us, length us, event | category | flops | bytes accessed | tf_op | source)
XLA Modules:
  0.0 57.0 jit_solution(15468053542566029851)
XLA Ops:
  0.6 2.1 %collective-permute-start.1 = (bf16[512,1024]{1,0:T(8,128)(2,1)}, bf16[512,1024]{1,0:T(8,128)(2,1)S(1)}, u32[]{:S(2)}, u32[]{:S(2)}) collective-permute-start(bf16[512,1024]{1,0:T(8,128)(2,1)} %refs_0_.1), channel_id=1, source_target_pairs={{0,1},{1,0},{2,3},{3,2},{4,5},{5,4},{6,7},{7,6},{8,9},{9,8},{10,11... | collective-permute-start | bytes 3145736 | tf_op jit(solution)/shard_map/ppermute | solution.py:550
  2.8 0.0 copy-start
  2.8 22.4 %input_grad_partials.1 = (bf16[512,1024]{1,0:T(8,128)(2,1)S(1)}, bf16[1024,1024]{1,0:T(8,128)(2,1)S(1)}, f32[512,1024]{1,0:T(8,128)S(1)}, f32[128,128,128]{2,1,0...) custom-call(s32[1]{0:T(128)} %bitcast.2.here_ref, s32[1]{0:T(128)} %bitcast._.me_ref, ...), custom_call_target="tpu_custom_call" | custom-call | flops 17179869184 | bytes 41943040 | tf_op jit(solution)/shard_map/input_grad_partials/pallas_call | solution.py:232
  25.2 0.1 collective-permute-start
  25.9 0.0 collective-permute-done.1.refs_1_
  25.9 0.0 copy-done
  26.0 3.7 %kept_blocks.1 = (bf16[1024,1024]{1,0:T(8,128)(2,1)S(1)}, bf16[1040,128]{1,0:T(8,128)(2,1)S(1)}, bf16[1024,1024]{1,0:T(8,128)(2,1)S(1)}, bf16[1024,1024]{1,0:T(8,128)(2,1)S(1)}) custom-call(s32[1]{0:T(128)} %bitcast.2.here_ref, s32[8]{0:T(128)S(1)} %bitcast.7, f32[1]{0:T(128)S(6)} %copy.15.step_ref, ...), custom_call_target="tpu_custom_call", output_to_operand_aliasing={{0}: (5, {})} | custom-call | flops 268435456 | bytes 6291456 | tf_op jit(solution)/shard_map/kept_blocks/pallas_call | solution.py:277
  29.7 2.6 %collective-permute-start.4 = (bf16[1040,128]{1,0:T(8,128)(2,1)S(1)}, bf16[1040,128]{1,0:T(8,128)(2,1)S(1)}, u32[]{:S(2)}, u32[]{:S(2)}) collective-permute-start(bf16[1040,128]{1,0:T(8,128)(2,1)S(1)} %get-tuple-element.21.refs_2_), channel_id=1, source_target_pairs={{0,24},{8,16},{16,8},{24,0},{1,25},{9,17},{17,9},{25,1},{2,26},{10... | collective-permute-start | bytes 798728 | tf_op jit(solution)/shard_map/ppermute | solution.py:550
  32.3 0.0 collective-permute-start.3
  32.3 0.5 collective-permute-start.2
  32.7 21.6 %residual_out.1.refs_7_ = bf16[1024,8192]{1,0:T(8,128)(2,1)} custom-call(s32[1]{0:T(128)} %bitcast.2.here_ref, f32[1]{0:T(128)S(6)} %copy.15.step_ref, bf16[1024,1024]{1,0:T(8,128)(2,1)S(1)} %get-tuple-element.23.acts_t_ref, bf16[1024,1024]{1,0:T(8,128)(2,1)S(1)} %get-tuple-element.24.cot_first, bf16[1024,1024]{1,0:T(8,128)(2,1)S(1)} %get-tuple-element.25.res_first, ...), custom_call_target="tpu_custom_call" | custom-call | flops 17179869184 | bytes 52428800 | tf_op jit(solution)/shard_map/residual_out/pallas_call | solution.py:401
  54.3 0.0 collective-permute-done.refs_1_
  54.3 0.0 collective-permute-done.4.refs_5_
  54.3 0.0 collective-permute-done.3.refs_4_
  54.4 0.0 collective-permute-done.2.refs_3_
  54.4 2.5 %finish.1 = (bf16[512,1024]{1,0:T(8,128)(2,1)}, f32[128,128,128]{2,1,0:T(8,128)}, bf16[1024,8192]{1,0:T(8,128)(2,1)}) custom-call(s32[1]{0:T(128)} %bitcast._.me_ref, s32[8]{0:T(128)S(1)} %bitcast.8, f32[512,1024]{1,0:T(8,128)S(1)} %get-tuple-element.16.refs_0_, ...), custom_call_target="tpu_custom_call", output_to_operand_aliasing={{1}: (8, {}), {2}: (9, {})} | custom-call | flops 524288 | bytes 4194304 | tf_op jit(solution)/shard_map/finish/pallas_call | solution.py:536
Async XLA Ops:
  0.6 25.3 %collective-permute-start.1 = (bf16[512,1024]{1,0:T(8,128)(2,1)}, bf16[512,1024]{1,0:T(8,128)(2,1)S(1)}, u32[]{:S(2)}, u32[]{:S(2)}) collective-permute-start(bf16[512,1024]{1,0:T(8,128)(2,1)} %refs_0_.1), channel_id=1, source_target_pairs={{0,1},{1,0},{2,3},{3,2},{4,5},{5,4},{6,7},{7,6},{8,9},{9,8},{10,11... | collective-permute-start | bytes 3145736 | tf_op jit(solution)/shard_map/ppermute | solution.py:550
  2.8 23.2 %copy-start = (s32[1,1,1,8]{3,2,1,0:T(1,128)S(1)}, s32[1,1,1,8]{3,2,1,0:T(1,128)}, u32[]{:S(2)}) copy-start(s32[1,1,1,8]{3,2,1,0:T(1,128)} %param.11) | copy-start | bytes 100
  25.2 29.1 %collective-permute-start = (bf16[512,1024]{1,0:T(8,128)(2,1)S(1)}, bf16[512,1024]{1,0:T(8,128)(2,1)S(1)}, u32[]{:S(2)}, u32[]{:S(2)}) collective-permute-start(bf16[512,1024]{1,0:T(8,128)(2,1)S(1)} %get-tuple-element.17), channel_id=1, source_target_pairs={{0,1},{1,0},{2,3},{3,2},{4,5},{5,4},{6,7},{7,6},{8,9},{9,8},{10,11... | collective-permute-start | bytes 3145736 | tf_op jit(solution)/shard_map/ppermute | solution.py:550
  29.7 24.7 %collective-permute-start.4 = (bf16[1040,128]{1,0:T(8,128)(2,1)S(1)}, bf16[1040,128]{1,0:T(8,128)(2,1)S(1)}, u32[]{:S(2)}, u32[]{:S(2)}) collective-permute-start(bf16[1040,128]{1,0:T(8,128)(2,1)S(1)} %get-tuple-element.21.refs_2_), channel_id=1, source_target_pairs={{0,24},{8,16},{16,8},{24,0},{1,25},{9,17},{17,9},{25,1},{2,26},{10... | collective-permute-start | bytes 798728 | tf_op jit(solution)/shard_map/ppermute | solution.py:550
  32.3 22.1 %collective-permute-start.3 = (bf16[1040,128]{1,0:T(8,128)(2,1)S(1)}, bf16[1040,128]{1,0:T(8,128)(2,1)S(1)}, u32[]{:S(2)}, u32[]{:S(2)}) collective-permute-start(bf16[1040,128]{1,0:T(8,128)(2,1)S(1)} %get-tuple-element.21.refs_2_), channel_id=1, source_target_pairs={{0,16},{8,24},{16,0},{24,8},{1,17},{9,25},{17,1},{25,9},{2,18},{10... | collective-permute-start | bytes 798728 | tf_op jit(solution)/shard_map/ppermute | solution.py:550
  32.3 22.1 %collective-permute-start.2 = (bf16[1040,128]{1,0:T(8,128)(2,1)S(1)}, bf16[1040,128]{1,0:T(8,128)(2,1)S(1)}, u32[]{:S(2)}, u32[]{:S(2)}) collective-permute-start(bf16[1040,128]{1,0:T(8,128)(2,1)S(1)} %get-tuple-element.21.refs_2_), channel_id=1, source_target_pairs={{0,8},{8,0},{16,24},{24,16},{1,9},{9,1},{17,25},{25,17},{2,10},{10... | collective-permute-start | bytes 798728 | tf_op jit(solution)/shard_map/ppermute | solution.py:550

commit v2 on v0

--- a/solution.py
+++ b/solution.py
@@ -65,14 +65,23 @@
     return pltpu.with_memory_space_constraint(x, pltpu.VMEM)
 
 
-def cot_copies(here_ref, split, cot_ref, buf_ref, sems):
+def row_copies(src_ref, dst_ref, sems, at=0, pieces=4):
+    rows = dst_ref.shape[0] // pieces
+    copies = []
+    for i in range(pieces):
+        part = pl.ds(i * rows, rows)
+        copies.append(pltpu.make_async_copy(src_ref.at[part], dst_ref.at[part], sems.at[at + i]))
+    return copies
+
+
+def cot_copies(here_ref, split, cot_ref, buf_ref, sems, pieces=4):
     if not split:
-        return [pltpu.make_async_copy(cot_ref, buf_ref, sems.at[0])]
+        return row_copies(cot_ref, buf_ref, sems, 0, pieces)
     half = buf_ref.shape[0] // 2
     copies = []
     for i, at in enumerate((here_ref[0], 1 - here_ref[0])):
         rows = pl.ds(pl.multiple_of(at * half, half), half)
-        copies.append(pltpu.make_async_copy(cot_ref.at[rows], buf_ref.at[pl.ds(i * half, half)], sems.at[i]))
+        copies += row_copies(cot_ref.at[rows], buf_ref.at[pl.ds(i * half, half)], sems, i * pieces // 2, pieces // 2)
     return copies
 
 
@@ -91,9 +100,9 @@
 
     def loads(at, size, cot_buf, w_buf, i):
         part = pl.ds(at, size)
-        return cot_copies(here_ref, split, cot_ref.at[:, part], cot_buf, cot_sem.at[i]) + [
-            pltpu.make_async_copy(w_ref.at[:, part], w_buf, w_sem.at[i])
-        ]
+        return cot_copies(here_ref, split, cot_ref.at[:, part], cot_buf, cot_sem.at[i]) + row_copies(
+            w_ref.at[:, part], w_buf, w_sem.at[i]
+        )
 
     def head_loads():
         return loads(0, head, cot_head, w_head, 0)
@@ -115,7 +124,7 @@
     def side_copies():
         part = pl.ds(0, res_first_ref.shape[1])
         copies = cot_copies(here_ref, split, cot_ref.at[:, part], cot_first_ref, first_sem)
-        copies.append(pltpu.make_async_copy(res_ref.at[:, part], res_first_ref, first_sem.at[2]))
+        copies += row_copies(res_ref.at[:, part], res_first_ref, first_sem, 4)
         for z in range(zero_copies):
             part = pl.ds(z * zero_rows, zero_rows)
             copies.append(pltpu.make_async_copy(zero_ref, owned_ref.at[part], zero_sem.at[z]))
@@ -123,7 +132,7 @@
             col_blocks = hidden // BLK
             row = pl.ds(pl.multiple_of(kept_ref[k] // col_blocks * BLK, BLK), BLK)
             col = pl.ds(pl.multiple_of(kept_ref[k] % col_blocks * BLK, BLK), BLK)
-            copies += cot_copies(here_ref, split, cot_ref.at[:, col], kept_cot_ref.at[k], kept_cot_sem.at[k])
+            copies += cot_copies(here_ref, split, cot_ref.at[:, col], kept_cot_ref.at[k], kept_cot_sem.at[k], 2)
             copies.append(pltpu.make_async_copy(res_ref.at[row, col], kept_res_ref.at[k], kept_res_sem.at[k]))
         return copies
 
@@ -219,12 +228,12 @@
         pltpu.VMEM((zero_rows, BLK, BLK), jnp.float32),
         pltpu.SMEM(kept.shape, jnp.int32),
         pltpu.SemaphoreType.DMA,
-        pltpu.SemaphoreType.DMA((chunks + 2, 2)),
-        pltpu.SemaphoreType.DMA((chunks + 2,)),
+        pltpu.SemaphoreType.DMA((chunks + 2, 4)),
+        pltpu.SemaphoreType.DMA((chunks + 2, 4)),
         pltpu.SemaphoreType.DMA((zero_copies,)),
         pltpu.SemaphoreType.DMA((keep, 2)),
         pltpu.SemaphoreType.DMA((keep,)),
-        pltpu.SemaphoreType.DMA((3,)),
+        pltpu.SemaphoreType.DMA((8,)),
         pltpu.SemaphoreType.DMA((4,)),
     ]
     if split:
@@ -300,12 +309,12 @@
 
     def loads(at, cot_buf, res_buf, i):
         part = pl.ds(at, res_buf.shape[1])
-        return cot_copies(here_ref, split, cot_ref.at[:, part], cot_buf, cot_sem.at[i]) + [
-            pltpu.make_async_copy(res_ref.at[:, part], res_buf, res_sem.at[i])
-        ]
+        return cot_copies(here_ref, split, cot_ref.at[:, part], cot_buf, cot_sem.at[i]) + row_copies(
+            res_ref.at[:, part], res_buf, res_sem.at[i]
+        )
 
     def store(at, res_buf, i):
-        return pltpu.make_async_copy(res_buf, out_ref.at[:, pl.ds(at, res_buf.shape[1])], out_sem.at[i])
+        return row_copies(res_buf, out_ref.at[:, pl.ds(at, res_buf.shape[1])], out_sem.at[i])
 
     def body_at(j):
         return pl.multiple_of(first + j * chunk, BLK)
@@ -351,7 +360,7 @@
         start_tails()
     work(cot_first, res_first, first_out)
     first_store = store(0, first_out, chunks + len(tails))
-    first_store.start()
+    start(first_store)
 
     if chunks:
         start(body_loads(1))
@@ -369,17 +378,17 @@
                 start_tails()
 
             work(cot_body.at[j], res_body.at[j], res_body.at[j])
-            body_store(j).start()
+            start(body_store(j))
 
     for t in range(len(tails)):
         wait(tail_loads(t))
         work(cot_tail.at[t], res_tail.at[t], res_tail.at[t])
-        tail_store(t).start()
-    first_store.wait()
+        start(tail_store(t))
+    wait(first_store)
     for j in range(chunks):
-        body_store(j).wait()
+        wait(body_store(j))
     for t in range(len(tails)):
-        tail_store(t).wait()
+        wait(tail_store(t))
 
 
 def residual_of(here, step_size, acts_t, cot_first, res_first, cot, residual, split):
@@ -398,9 +407,9 @@
             pltpu.VMEM((max(chunks, 1), rows, chunk), jnp.bfloat16),
             pltpu.VMEM((len(tails), tokens, tails[0]), jnp.bfloat16),
             pltpu.VMEM((len(tails), rows, tails[0]), jnp.bfloat16),
-            pltpu.SemaphoreType.DMA((parts, 2)),
-            pltpu.SemaphoreType.DMA((parts,)),
-            pltpu.SemaphoreType.DMA((parts + 1,)),
+            pltpu.SemaphoreType.DMA((parts, 4)),
+            pltpu.SemaphoreType.DMA((parts, 4)),
+            pltpu.SemaphoreType.DMA((parts + 1, 4)),
         ],
         compiler_params=params(36),
         cost_estimate=cost(2 * tokens * rows * cols, 2 * tokens * (rows + cols) + 4 * rows * cols),

time: 55.5 us -> 57.2 us (1.031)
  Pallas kernels: 47.9 us -> 50 us
    pallas_call x1, Pallas kernels: 20.6 us -> 21.9 us  [residual_of(): pl.pallas_call(functools.partial(residual_kernel, split), out_shape=pltpu...]
    pallas_call x1, Pallas kernels: 23.2 us -> 24 us  [input_grad_partials(): pl.pallas_call(functools.partial(input_grad_kernel, split, zero_copies),...]
  transfers between devices with their start and end apart: 5 -> 5, of which waited for: 0 -> 0; matrix products, arithmetic and copies ran while one was open for 0% -> 0% of each run, Pallas kernels for 83% -> 84%
where the time goes in v2:
time: 57.2 us; the launch traced here: 56.8 us
  Pallas kernels  50 us (87%)
  starting transfers between devices  5.29 us (9%)
  between operations  1.51 us (3%)
    pallas_call x1, Pallas kernels, input_grad_partials(): pl.pallas_call(functools.partial(input_grad_kernel, split, zero_copies),...  24 us
    pallas_call x1, Pallas kernels, residual_of(): pl.pallas_call(functools.partial(residual_kernel, split), out_shape=pltpu...  21.9 us
    ppermute x5, starting transfers between devices, swapped(): lax.ppermute(x, axis, [(i, i ^ mask) for i in range(lax.axis_size(axis))])  5.29 us
    pallas_call x1, Pallas kernels, finish(): pl.pallas_call(functools.partial(finish_kernel, groups, keep, bool(parts)...  2.51 us
    pallas_call x1, Pallas kernels, kept_blocks_of(): pl.pallas_call(functools.partial(kept_kernel, pair, col_blocks), out_shap...  1.58 us
  transfers between devices with their start and end apart: 5, of which 0 were waited for; matrix products, arithmetic and copies ran while one was open for 0% of the time, Pallas kernels for 84%

profile of v2, /device:TPU:1, one launch (start us, length us, event | category | flops | bytes accessed | tf_op | source)
XLA Modules:
  0.0 56.8 jit_solution(875966929052800075)
XLA Ops:
  0.6 2.1 %collective-permute-start.1 = (bf16[512,1024]{1,0:T(8,128)(2,1)}, bf16[512,1024]{1,0:T(8,128)(2,1)S(1)}, u32[]{:S(2)}, u32[]{:S(2)}) collective-permute-start(bf16[512,1024]{1,0:T(8,128)(2,1)} %refs_0_.1), channel_id=1, source_target_pairs={{0,1},{1,0},{2,3},{3,2},{4,5},{5,4},{6,7},{7,6},{8,9},{9,8},{10,11... | collective-permute-start | bytes 3145736 | tf_op jit(solution)/shard_map/ppermute | solution.py:548
  2.8 0.0 copy-start
  2.8 24.0 %input_grad_partials.1 = (bf16[512,1024]{1,0:T(8,128)(2,1)}, bf16[1024,1024]{1,0:T(8,128)(2,1)S(1)}, f32[512,1024]{1,0:T(8,128)S(1)}, f32[128,128,128]{2,1,0:T(8...) custom-call(s32[1]{0:T(128)} %bitcast.2.here_ref, ...), custom_call_target="tpu_custom_call" | custom-call | flops 17179869184 | bytes 41943040 | tf_op jit(solution)/shard_map/input_grad_partials/pallas_call | solution.py:253
  26.8 0.1 collective-permute-start
  27.6 0.0 collective-permute-done.1.refs_1_
  27.6 0.0 copy-done
  27.6 1.6 %kept_blocks.1 = (bf16[1024,1024]{1,0:T(8,128)(2,1)S(1)}, bf16[1040,128]{1,0:T(8,128)(2,1)S(1)}) custom-call(s32[8]{0:T(128)S(1)} %bitcast.7, f32[1]{0:T(128)S(6)} %copy.15.step_ref, bf16[1024,1024]{1,0:T(8,128)(2,1)S(1)} %get-tuple-element.18.refs_0_, bf16[512,1024]{1,0:T(8,128)(2,1)S(1)} %collective-permute-done.1.refs_1_, ...), custom_call_target="tpu_custom_call", output_to_operand_aliasing={{0}: (2, {})} | custom-call | flops 268435456 | bytes 6291456 | tf_op jit(solution)/shard_map/kept_blocks/pallas_call | solution.py:290
  29.2 2.6 %collective-permute-start.4 = (bf16[1040,128]{1,0:T(8,128)(2,1)S(1)}, bf16[1040,128]{1,0:T(8,128)(2,1)S(1)}, u32[]{:S(2)}, u32[]{:S(2)}) collective-permute-start(bf16[1040,128]{1,0:T(8,128)(2,1)S(1)} %get-tuple-element.21.refs_2_), channel_id=1, source_target_pairs={{0,24},{8,16},{16,8},{24,0},{1,25},{9,17},{17,9},{25,1},{2,26},{10... | collective-permute-start | bytes 798728 | tf_op jit(solution)/shard_map/ppermute | solution.py:548
  31.8 0.0 collective-permute-start.3
  31.8 0.5 collective-permute-start.2
  32.2 21.9 %residual_out.1.refs_7_ = bf16[1024,8192]{1,0:T(8,128)(2,1)} custom-call(s32[1]{0:T(128)} %bitcast.2.here_ref, f32[1]{0:T(128)S(6)} %copy.15.step_ref, bf16[1024,1024]{1,0:T(8,128)(2,1)S(1)} %get-tuple-element.23.acts_t_ref, bf16[1024,1024]{1,0:T(8,128)(2,1)S(1)} %get-tuple-element.24.cot_first, bf16[1024,1024]{1,0:T(8,128)(2,1)S(1)} %get-tuple-element.25.res_first, ...), custom_call_target="tpu_custom_call" | custom-call | flops 17179869184 | bytes 52428800 | tf_op jit(solution)/shard_map/residual_out/pallas_call | solution.py:399
  54.1 0.0 collective-permute-done.refs_1_
  54.1 0.0 collective-permute-done.4.refs_5_
  54.1 0.0 collective-permute-done.3.refs_4_
  54.1 0.0 collective-permute-done.2.refs_3_
  54.1 2.5 %finish.1 = (bf16[512,1024]{1,0:T(8,128)(2,1)}, f32[128,128,128]{2,1,0:T(8,128)}, bf16[1024,8192]{1,0:T(8,128)(2,1)}) custom-call(s32[1]{0:T(128)} %bitcast._.me_ref, s32[8]{0:T(128)S(1)} %bitcast.8, f32[512,1024]{1,0:T(8,128)S(1)} %get-tuple-element.16.refs_0_, ...), custom_call_target="tpu_custom_call", output_to_operand_aliasing={{1}: (8, {}), {2}: (9, {})} | custom-call | flops 524288 | bytes 4194304 | tf_op jit(solution)/shard_map/finish/pallas_call | solution.py:534
Async XLA Ops:
  0.6 26.9 %collective-permute-start.1 = (bf16[512,1024]{1,0:T(8,128)(2,1)}, bf16[512,1024]{1,0:T(8,128)(2,1)S(1)}, u32[]{:S(2)}, u32[]{:S(2)}) collective-permute-start(bf16[512,1024]{1,0:T(8,128)(2,1)} %refs_0_.1), channel_id=1, source_target_pairs={{0,1},{1,0},{2,3},{3,2},{4,5},{5,4},{6,7},{7,6},{8,9},{9,8},{10,11... | collective-permute-start | bytes 3145736 | tf_op jit(solution)/shard_map/ppermute | solution.py:548
  2.8 24.8 %copy-start = (s32[1,1,1,8]{3,2,1,0:T(1,128)S(1)}, s32[1,1,1,8]{3,2,1,0:T(1,128)}, u32[]{:S(2)}) copy-start(s32[1,1,1,8]{3,2,1,0:T(1,128)} %param.11) | copy-start | bytes 100
  26.8 27.3 %collective-permute-start = (bf16[512,1024]{1,0:T(8,128)(2,1)}, bf16[512,1024]{1,0:T(8,128)(2,1)S(1)}, u32[]{:S(2)}, u32[]{:S(2)}) collective-permute-start(bf16[512,1024]{1,0:T(8,128)(2,1)} %get-tuple-element.17), channel_id=1, source_target_pairs={{0,1},{1,0},{2,3},{3,2},{4,5},{5,4},{6,7},{7,6},{8,9},{9,8},{10,11... | collective-permute-start | bytes 3145736 | tf_op jit(solution)/shard_map/ppermute | solution.py:548
  29.2 24.9 %collective-permute-start.4 = (bf16[1040,128]{1,0:T(8,128)(2,1)S(1)}, bf16[1040,128]{1,0:T(8,128)(2,1)S(1)}, u32[]{:S(2)}, u32[]{:S(2)}) collective-permute-start(bf16[1040,128]{1,0:T(8,128)(2,1)S(1)} %get-tuple-element.21.refs_2_), channel_id=1, source_target_pairs={{0,24},{8,16},{16,8},{24,0},{1,25},{9,17},{17,9},{25,1},{2,26},{10... | collective-permute-start | bytes 798728 | tf_op jit(solution)/shard_map/ppermute | solution.py:548
  31.8 22.4 %collective-permute-start.3 = (bf16[1040,128]{1,0:T(8,128)(2,1)S(1)}, bf16[1040,128]{1,0:T(8,128)(2,1)S(1)}, u32[]{:S(2)}, u32[]{:S(2)}) collective-permute-start(bf16[1040,128]{1,0:T(8,128)(2,1)S(1)} %get-tuple-element.21.refs_2_), channel_id=1, source_target_pairs={{0,16},{8,24},{16,0},{24,8},{1,17},{9,25},{17,1},{25,9},{2,18},{10... | collective-permute-start | bytes 798728 | tf_op jit(solution)/shard_map/ppermute | solution.py:548
  31.8 22.4 %collective-permute-start.2 = (bf16[1040,128]{1,0:T(8,128)(2,1)S(1)}, bf16[1040,128]{1,0:T(8,128)(2,1)S(1)}, u32[]{:S(2)}, u32[]{:S(2)}) collective-permute-start(bf16[1040,128]{1,0:T(8,128)(2,1)S(1)} %get-tuple-element.21.refs_2_), channel_id=1, source_target_pairs={{0,8},{8,0},{16,24},{24,16},{1,9},{9,1},{17,25},{25,17},{2,10},{10... | collective-permute-start | bytes 798728 | tf_op jit(solution)/shard_map/ppermute | solution.py:548
